TPU v7x, 512 devices: a whole 4x4x16 slice. The times are simulated.
512 devices in a mesh: stn: 32 (over z_lo, y), tm: 16 (over z_hi, x, core).
Axes of the slice: x: 4, y: 4, z: 16 (z_hi: 2, z_lo: 8; z = z_hi * 8 + z_lo), core: 2. Of those that a mesh axis runs over, the one named last changes fastest.
Arguments:
- voltages: bfloat16 [2, 128, 393216], P(None, 'stn', 'tm'), may hold values from -20 to 20, as said below
Outputs:
- visibilities: float32 [2, 128, 128, 4096], P(None, 'stn', None, 'tm')
Inputs may be any that keep to these rules, and one draw needn't show every extreme that they name: `voltages`: voltage samples.
All inputs are finite; a program needn't handle non-finite values.
Results may differ from a plain program's by a relative error of at most 0.0018.
Values may be sent and summed in bfloat16 or wider, within the bound.
No kernel may reach another device: no remote copies, remote signals or barrier semaphores. Data moves between devices by JAX's collectives and lax.ppermute only.
A program may use at most 128 MiB of HBM per device.

v0:
```python
import math
import jax
import jax.numpy as jnp
from jax import lax
from jax.sharding import PartitionSpec as P

TAPS = 16
RADIX = 64
NCH = 4096


def passed_along(value, axis, steps):
    count = lax.axis_size(axis)
    leading, last = (max(0, -steps), min(count, count - steps))
    return lax.ppermute(value, axis, [(source, source + steps) for source in range(leading, last)])


def from_behind(x, axis, by):
    count = lax.axis_size(axis)
    return lax.ppermute(x, axis, [(i, (i + by) % count) for i in range(count)])


def prototype():
    total = TAPS * NCH
    index = jnp.arange(total).astype(jnp.float32)
    offset = (index + 0.5 - total / 2.0) / NCH
    window = 0.5 - 0.5 * jnp.cos(2.0 * math.pi * (index + 0.5) / total)
    return (jnp.sinc(offset) * window).reshape(TAPS, NCH)


def rotation_block(order):
    index = jnp.arange(order, dtype=jnp.int32)
    angle = 2.0 * math.pi * (index[:, None] * index[None, :] % order).astype(jnp.float32) / order
    cosine = jnp.cos(angle)
    sine = jnp.sin(angle)
    upper = jnp.concatenate([cosine, -sine], 1)
    lower = jnp.concatenate([sine, cosine], 1)
    return jnp.concatenate([upper, lower], 0)


def transform(filtered):
    inputs_dev = filtered.shape[1]
    frames_dev = filtered.shape[2]
    radix = RADIX
    table = rotation_block(radix)
    index = jnp.arange(radix, dtype=jnp.int32)
    angle = 2.0 * math.pi * (index[:, None] * index[None, :] % NCH).astype(jnp.float32) / NCH
    cos_pair = jnp.concatenate([jnp.cos(angle), jnp.cos(angle)], 1)
    sin_pair = jnp.concatenate([jnp.sin(angle), jnp.sin(angle)], 1)
    values = filtered.astype(jnp.float32).reshape(2, inputs_dev, frames_dev, radix, radix)
    values = jnp.transpose(values, (1, 2, 4, 0, 3)).reshape(
        inputs_dev, frames_dev, radix, 2 * radix
    )
    section = jnp.einsum("ifbk,kl->ifbl", values, table, precision=lax.Precision.HIGHEST)
    swapped = jnp.concatenate([section[..., radix:], -section[..., :radix]], -1)
    twisted = section * cos_pair + swapped * sin_pair
    twisted = twisted.reshape(inputs_dev, frames_dev, radix, 2, radix)
    twisted = jnp.transpose(twisted, (0, 1, 4, 3, 2)).reshape(
        inputs_dev, frames_dev, radix, 2 * radix
    )
    second = jnp.einsum("ifbk,kl->ifbl", twisted, table, precision=lax.Precision.HIGHEST)
    second = second.reshape(inputs_dev, frames_dev, radix, 2, radix)
    second = jnp.transpose(second, (3, 0, 1, 4, 2)).reshape(2, inputs_dev, frames_dev, NCH)
    return (second / radix).astype(jnp.bfloat16)


def shards(voltages):
    taps_table = prototype()
    inputs_dev = voltages.shape[1]
    frames_dev = voltages.shape[2] // NCH
    reach = (TAPS - 2) // frames_dev + 1
    earlier = []
    for distance in range(reach, 0, -1):
        earlier.append(passed_along(voltages, "tm", distance))
    before = jnp.concatenate(earlier, 2)
    history = before[:, :, before.shape[2] - (TAPS - 1) * NCH :]
    joined = jnp.concatenate([history, voltages], 2).astype(jnp.float32)
    joined = joined.reshape(2, inputs_dev, frames_dev + TAPS - 1, NCH)
    filtered = jnp.zeros((2, inputs_dev, frames_dev, NCH), jnp.float32)
    for tap in range(TAPS):
        filtered = filtered + joined[:, :, tap : tap + frames_dev, :] * taps_table[tap]
    spectra = transform(filtered.astype(jnp.bfloat16))
    turned = lax.all_to_all(spectra, "tm", split_axis=3, concat_axis=2, tiled=True)
    frames_all = turned.shape[2]
    width = turned.shape[3]
    count = lax.axis_size("stn")
    here = lax.axis_index("stn")
    zero_at = jnp.zeros((), jnp.int32)
    blank = jnp.zeros((2, inputs_dev, inputs_dev * count, width), jnp.float32)

    def correlate(other):
        products = jnp.einsum("aifc,bjfc->abijc", turned, other, preferred_element_type=jnp.float32)
        real_part = products[0, 0] + products[1, 1]
        imag_part = products[1, 0] - products[0, 1]
        return jnp.stack([real_part, imag_part]) / frames_all

    def place(accum, block, group):
        start = group * inputs_dev
        return lax.dynamic_update_slice(accum, block, (zero_at, zero_at, start, zero_at))

    accum = place(blank, correlate(turned), here)

    def advance_step(step, carry):
        moving, accum = carry
        moving = from_behind(moving, "stn", 1)
        group = (here - step) % count
        return (moving, place(accum, correlate(moving), group))

    moving, accum = lax.fori_loop(1, count, advance_step, (turned, accum))
    return accum


def solution(mesh):
    in_specs = (P(None, "stn", "tm"),)
    out_specs = P(None, "stn", None, "tm")
    return jax.shard_map(shards, mesh=mesh, in_specs=in_specs, out_specs=out_specs, check_vma=False)
```

profile of v0, /device:TPU:2, one launch (start us, length us, event | category | flops | bytes accessed | tf_op | source)
XLA Modules:
  0.0 1016.9 jit_solution(4058024477677042663)
XLA Ops:
  6.0 14.9 %collective-permute-start.3 = (bf16[2,4,24576]{2,1,0:T(4,128)(2,1)}, bf16[2,4,24576]{2,1,0:T(4,128)(2,1)S(1)}, u32[]{:S(2)}, u32[]{:S(2)}) collective-permute-start(bf16[2,4,24576]{2,1,0:T(4,128)(2,1)} %param.3), channel_id=1, source_target_pairs={{0,1},{1,2},{2,3},{3,4},{4,5},{5,6},{6,7},{7,8},{8,9},{9,10},{10,1... | collective-permute-start | bytes 1179656 | tf_op jit(solution)/shard_map/ppermute | solution.py:15
  43.8 14.1 %copy.78 = bf16[2,4,6,64,64]{2,1,0,4,3:T(4,128)(2,1)} copy(bf16[2,4,6,64,64]{3,4,0,2,1:T(8,128)(2,1)S(1)} %fusion.7) | data formatting | bytes 786432 | tf_op jit(solution)/shard_map/convert_element_type | solution.py:64
  58.0 14.3 %reshape.178 = bf16[16,2,6144]{2,1,0:T(2,128)(2,1)} reshape(bf16[4096,2,4,6]{3,2,1,0:T(4,128)(2,1)} %bitcast.66) | data formatting | bytes 786432
  72.3 25.2 %all-to-all-start = ((bf16[16,2,6144]{2,1,0:T(2,128)(2,1)}), bf16[16,2,6144]{2,1,0:T(2,128)(2,1)S(1)}, u32[]{:S(2)}, u32[]{:S(2)}) async-start(bf16[16,2,6144]{2,1,0:T(2,128)(2,1)} %reshape.178), calls=%async_computation | async-start | bytes 786432 | tf_op jit(solution)/shard_map/all_to_all | solution.py:83
  97.5 15.0 %all-to-all-done = bf16[16,2,6144]{2,1,0:T(2,128)(2,1)S(1)} async-done(((bf16[16,2,6144]{2,1,0:T(2,128)(2,1)}), bf16[16,2,6144]{2,1,0:T(2,128)(2,1)S(1)}, u32[]{:S(2)}, u32[]{:S(2)}) %all-to-all-start) | async-done | bytes 393248 | tf_op jit(solution)/shard_map/all_to_all | solution.py:83
  112.5 20.0 %reshape.179 = bf16[4096,2,4,6]{3,2,1,0:T(4,128)(2,1)} reshape(bf16[16,2,6144]{2,1,0:T(2,128)(2,1)S(1)} %all-to-all-done) | data formatting | bytes 786432
  132.5 8.8 copy.79
  142.7 4.7 convolution_bitcast_fusion.1
  149.0 866.9 %while.17 = (s32[]{:T(128)}, bf16[2,4,96,256]{2,1,0,3:T(4,128)(2,1)S(1)}, f32[2,4,128,256]{3,2,1,0:T(8,128)S(1)}, bf16[2,4,96,256]{2,1,0,3:T(4,128)(2,1)S(1)}, s...) while((s32[]{:T(128)}, ...), condition=%wide.region_1.2_spmd, body=%wide.region_0.1_spmd.sunk | while | flops 3170322 | bytes 3440960 | solution.py:109
  152.5 21.8 %collective-permute-done = bf16[2,4,96,256]{2,1,0,3:T(4,128)(2,1)S(1)} collective-permute-done((bf16[2,4,96,256]{2,1,0,3:T(4,128)(2,1)S(1)}, bf16[2,4,96,256]{2,1,0,3:T(4,128)(2,1)S(1)}, u32[]{:S(2)}, u32[]{:S(2)}) %collective-permute-start) | collective-permute-done | bytes 393248 | tf_op jit(solution)/shard_map/while/body/eval_jaxpr/ppermute | solution.py:20
  174.3 4.7 convolution_bitcast_fusion.3
  181.9 22.3 %collective-permute-done = bf16[2,4,96,256]{2,1,0,3:T(4,128)(2,1)S(1)} collective-permute-done((bf16[2,4,96,256]{2,1,0,3:T(4,128)(2,1)S(1)}, bf16[2,4,96,256]{2,1,0,3:T(4,128)(2,1)S(1)}, u32[]{:S(2)}, u32[]{:S(2)}) %collective-permute-start) | collective-permute-done | bytes 393248 | tf_op jit(solution)/shard_map/while/body/eval_jaxpr/ppermute | solution.py:20
  204.2 4.7 convolution_bitcast_fusion.3
  211.8 21.4 %collective-permute-done = bf16[2,4,96,256]{2,1,0,3:T(4,128)(2,1)S(1)} collective-permute-done((bf16[2,4,96,256]{2,1,0,3:T(4,128)(2,1)S(1)}, bf16[2,4,96,256]{2,1,0,3:T(4,128)(2,1)S(1)}, u32[]{:S(2)}, u32[]{:S(2)}) %collective-permute-start) | collective-permute-done | bytes 393248 | tf_op jit(solution)/shard_map/while/body/eval_jaxpr/ppermute | solution.py:20
  233.2 4.7 convolution_bitcast_fusion.3
  238.9 36.5 %collective-permute-start = (bf16[2,4,96,256]{2,1,0,3:T(4,128)(2,1)S(1)}, bf16[2,4,96,256]{2,1,0,3:T(4,128)(2,1)S(1)}, u32[]{:S(2)}, u32[]{:S(2)}) collective-permute-start(bf16[2,4,96,256]{2,1,0,3:T(4,128)(2,1)S(1)} %get-tuple-element.242), channel_id=1, source_target_pairs={{0,16},{16,32},{32,48},{48,64},{64,80},{80,96},{96,112},{112,128},... | collective-permute-start | bytes 1179656 | tf_op jit(solution)/shard_map/while/body/eval_jaxpr/ppermute | solution.py:20
  275.4 9.4 collective-permute-done
  290.4 6.5 collective-permute-start
  297.0 16.5 %collective-permute-done = bf16[2,4,96,256]{2,1,0,3:T(4,128)(2,1)S(1)} collective-permute-done((bf16[2,4,96,256]{2,1,0,3:T(4,128)(2,1)S(1)}, bf16[2,4,96,256]{2,1,0,3:T(4,128)(2,1)S(1)}, u32[]{:S(2)}, u32[]{:S(2)}) %collective-permute-start) | collective-permute-done | bytes 393248 | tf_op jit(solution)/shard_map/while/body/eval_jaxpr/ppermute | solution.py:20
  313.4 4.7 convolution_bitcast_fusion.3
  321.1 20.1 %collective-permute-done = bf16[2,4,96,256]{2,1,0,3:T(4,128)(2,1)S(1)} collective-permute-done((bf16[2,4,96,256]{2,1,0,3:T(4,128)(2,1)S(1)}, bf16[2,4,96,256]{2,1,0,3:T(4,128)(2,1)S(1)}, u32[]{:S(2)}, u32[]{:S(2)}) %collective-permute-start) | collective-permute-done | bytes 393248 | tf_op jit(solution)/shard_map/while/body/eval_jaxpr/ppermute | solution.py:20
  341.2 4.7 convolution_bitcast_fusion.3
  348.8 19.2 %collective-permute-done = bf16[2,4,96,256]{2,1,0,3:T(4,128)(2,1)S(1)} collective-permute-done((bf16[2,4,96,256]{2,1,0,3:T(4,128)(2,1)S(1)}, bf16[2,4,96,256]{2,1,0,3:T(4,128)(2,1)S(1)}, u32[]{:S(2)}, u32[]{:S(2)}) %collective-permute-start) | collective-permute-done | bytes 393248 | tf_op jit(solution)/shard_map/while/body/eval_jaxpr/ppermute | solution.py:20
  368.0 4.7 convolution_bitcast_fusion.3
  375.6 18.3 %collective-permute-done = bf16[2,4,96,256]{2,1,0,3:T(4,128)(2,1)S(1)} collective-permute-done((bf16[2,4,96,256]{2,1,0,3:T(4,128)(2,1)S(1)}, bf16[2,4,96,256]{2,1,0,3:T(4,128)(2,1)S(1)}, u32[]{:S(2)}, u32[]{:S(2)}) %collective-permute-start) | collective-permute-done | bytes 393248 | tf_op jit(solution)/shard_map/while/body/eval_jaxpr/ppermute | solution.py:20
  401.5 17.8 %collective-permute-done = bf16[2,4,96,256]{2,1,0,3:T(4,128)(2,1)S(1)} collective-permute-done((bf16[2,4,96,256]{2,1,0,3:T(4,128)(2,1)S(1)}, bf16[2,4,96,256]{2,1,0,3:T(4,128)(2,1)S(1)}, u32[]{:S(2)}, u32[]{:S(2)}) %collective-permute-start) | collective-permute-done | bytes 393248 | tf_op jit(solution)/shard_map/while/body/eval_jaxpr/ppermute | solution.py:20
  426.9 17.8 %collective-permute-done = bf16[2,4,96,256]{2,1,0,3:T(4,128)(2,1)S(1)} collective-permute-done((bf16[2,4,96,256]{2,1,0,3:T(4,128)(2,1)S(1)}, bf16[2,4,96,256]{2,1,0,3:T(4,128)(2,1)S(1)}, u32[]{:S(2)}, u32[]{:S(2)}) %collective-permute-start) | collective-permute-done | bytes 393248 | tf_op jit(solution)/shard_map/while/body/eval_jaxpr/ppermute | solution.py:20
  452.4 17.8 %collective-permute-done = bf16[2,4,96,256]{2,1,0,3:T(4,128)(2,1)S(1)} collective-permute-done((bf16[2,4,96,256]{2,1,0,3:T(4,128)(2,1)S(1)}, bf16[2,4,96,256]{2,1,0,3:T(4,128)(2,1)S(1)}, u32[]{:S(2)}, u32[]{:S(2)}) %collective-permute-start) | collective-permute-done | bytes 393248 | tf_op jit(solution)/shard_map/while/body/eval_jaxpr/ppermute | solution.py:20
  477.8 17.8 %collective-permute-done = bf16[2,4,96,256]{2,1,0,3:T(4,128)(2,1)S(1)} collective-permute-done((bf16[2,4,96,256]{2,1,0,3:T(4,128)(2,1)S(1)}, bf16[2,4,96,256]{2,1,0,3:T(4,128)(2,1)S(1)}, u32[]{:S(2)}, u32[]{:S(2)}) %collective-permute-start) | collective-permute-done | bytes 393248 | tf_op jit(solution)/shard_map/while/body/eval_jaxpr/ppermute | solution.py:20
  503.2 17.8 %collective-permute-done = bf16[2,4,96,256]{2,1,0,3:T(4,128)(2,1)S(1)} collective-permute-done((bf16[2,4,96,256]{2,1,0,3:T(4,128)(2,1)S(1)}, bf16[2,4,96,256]{2,1,0,3:T(4,128)(2,1)S(1)}, u32[]{:S(2)}, u32[]{:S(2)}) %collective-permute-start) | collective-permute-done | bytes 393248 | tf_op jit(solution)/shard_map/while/body/eval_jaxpr/ppermute | solution.py:20
  528.7 17.8 %collective-permute-done = bf16[2,4,96,256]{2,1,0,3:T(4,128)(2,1)S(1)} collective-permute-done((bf16[2,4,96,256]{2,1,0,3:T(4,128)(2,1)S(1)}, bf16[2,4,96,256]{2,1,0,3:T(4,128)(2,1)S(1)}, u32[]{:S(2)}, u32[]{:S(2)}) %collective-permute-start) | collective-permute-done | bytes 393248 | tf_op jit(solution)/shard_map/while/body/eval_jaxpr/ppermute | solution.py:20
  554.1 17.8 %collective-permute-done = bf16[2,4,96,256]{2,1,0,3:T(4,128)(2,1)S(1)} collective-permute-done((bf16[2,4,96,256]{2,1,0,3:T(4,128)(2,1)S(1)}, bf16[2,4,96,256]{2,1,0,3:T(4,128)(2,1)S(1)}, u32[]{:S(2)}, u32[]{:S(2)}) %collective-permute-start) | collective-permute-done | bytes 393248 | tf_op jit(solution)/shard_map/while/body/eval_jaxpr/ppermute | solution.py:20
  579.6 17.8 %collective-permute-done = bf16[2,4,96,256]{2,1,0,3:T(4,128)(2,1)S(1)} collective-permute-done((bf16[2,4,96,256]{2,1,0,3:T(4,128)(2,1)S(1)}, bf16[2,4,96,256]{2,1,0,3:T(4,128)(2,1)S(1)}, u32[]{:S(2)}, u32[]{:S(2)}) %collective-permute-start) | collective-permute-done | bytes 393248 | tf_op jit(solution)/shard_map/while/body/eval_jaxpr/ppermute | solution.py:20
  605.0 17.8 %collective-permute-done = bf16[2,4,96,256]{2,1,0,3:T(4,128)(2,1)S(1)} collective-permute-done((bf16[2,4,96,256]{2,1,0,3:T(4,128)(2,1)S(1)}, bf16[2,4,96,256]{2,1,0,3:T(4,128)(2,1)S(1)}, u32[]{:S(2)}, u32[]{:S(2)}) %collective-permute-start) | collective-permute-done | bytes 393248 | tf_op jit(solution)/shard_map/while/body/eval_jaxpr/ppermute | solution.py:20
  630.4 17.8 %collective-permute-done = bf16[2,4,96,256]{2,1,0,3:T(4,128)(2,1)S(1)} collective-permute-done((bf16[2,4,96,256]{2,1,0,3:T(4,128)(2,1)S(1)}, bf16[2,4,96,256]{2,1,0,3:T(4,128)(2,1)S(1)}, u32[]{:S(2)}, u32[]{:S(2)}) %collective-permute-start) | collective-permute-done | bytes 393248 | tf_op jit(solution)/shard_map/while/body/eval_jaxpr/ppermute | solution.py:20
  655.9 17.8 %collective-permute-done = bf16[2,4,96,256]{2,1,0,3:T(4,128)(2,1)S(1)} collective-permute-done((bf16[2,4,96,256]{2,1,0,3:T(4,128)(2,1)S(1)}, bf16[2,4,96,256]{2,1,0,3:T(4,128)(2,1)S(1)}, u32[]{:S(2)}, u32[]{:S(2)}) %collective-permute-start) | collective-permute-done | bytes 393248 | tf_op jit(solution)/shard_map/while/body/eval_jaxpr/ppermute | solution.py:20
  681.3 17.8 %collective-permute-done = bf16[2,4,96,256]{2,1,0,3:T(4,128)(2,1)S(1)} collective-permute-done((bf16[2,4,96,256]{2,1,0,3:T(4,128)(2,1)S(1)}, bf16[2,4,96,256]{2,1,0,3:T(4,128)(2,1)S(1)}, u32[]{:S(2)}, u32[]{:S(2)}) %collective-permute-start) | collective-permute-done | bytes 393248 | tf_op jit(solution)/shard_map/while/body/eval_jaxpr/ppermute | solution.py:20
  706.8 18.9 %collective-permute-done = bf16[2,4,96,256]{2,1,0,3:T(4,128)(2,1)S(1)} collective-permute-done((bf16[2,4,96,256]{2,1,0,3:T(4,128)(2,1)S(1)}, bf16[2,4,96,256]{2,1,0,3:T(4,128)(2,1)S(1)}, u32[]{:S(2)}, u32[]{:S(2)}) %collective-permute-start) | collective-permute-done | bytes 393248 | tf_op jit(solution)/shard_map/while/body/eval_jaxpr/ppermute | solution.py:20
  733.3 20.0 %collective-permute-done = bf16[2,4,96,256]{2,1,0,3:T(4,128)(2,1)S(1)} collective-permute-done((bf16[2,4,96,256]{2,1,0,3:T(4,128)(2,1)S(1)}, bf16[2,4,96,256]{2,1,0,3:T(4,128)(2,1)S(1)}, u32[]{:S(2)}, u32[]{:S(2)}) %collective-permute-start) | collective-permute-done | bytes 393248 | tf_op jit(solution)/shard_map/while/body/eval_jaxpr/ppermute | solution.py:20
  760.9 21.1 %collective-permute-done = bf16[2,4,96,256]{2,1,0,3:T(4,128)(2,1)S(1)} collective-permute-done((bf16[2,4,96,256]{2,1,0,3:T(4,128)(2,1)S(1)}, bf16[2,4,96,256]{2,1,0,3:T(4,128)(2,1)S(1)}, u32[]{:S(2)}, u32[]{:S(2)}) %collective-permute-start) | collective-permute-done | bytes 393248 | tf_op jit(solution)/shard_map/while/body/eval_jaxpr/ppermute | solution.py:20
  789.6 22.2 %collective-permute-done = bf16[2,4,96,256]{2,1,0,3:T(4,128)(2,1)S(1)} collective-permute-done((bf16[2,4,96,256]{2,1,0,3:T(4,128)(2,1)S(1)}, bf16[2,4,96,256]{2,1,0,3:T(4,128)(2,1)S(1)}, u32[]{:S(2)}, u32[]{:S(2)}) %collective-permute-start) | collective-permute-done | bytes 393248 | tf_op jit(solution)/shard_map/while/body/eval_jaxpr/ppermute | solution.py:20
  819.4 23.3 %collective-permute-done = bf16[2,4,96,256]{2,1,0,3:T(4,128)(2,1)S(1)} collective-permute-done((bf16[2,4,96,256]{2,1,0,3:T(4,128)(2,1)S(1)}, bf16[2,4,96,256]{2,1,0,3:T(4,128)(2,1)S(1)}, u32[]{:S(2)}, u32[]{:S(2)}) %collective-permute-start) | collective-permute-done | bytes 393248 | tf_op jit(solution)/shard_map/while/body/eval_jaxpr/ppermute | solution.py:20
  850.3 22.6 %collective-permute-done = bf16[2,4,96,256]{2,1,0,3:T(4,128)(2,1)S(1)} collective-permute-done((bf16[2,4,96,256]{2,1,0,3:T(4,128)(2,1)S(1)}, bf16[2,4,96,256]{2,1,0,3:T(4,128)(2,1)S(1)}, u32[]{:S(2)}, u32[]{:S(2)}) %collective-permute-start) | collective-permute-done | bytes 393248 | tf_op jit(solution)/shard_map/while/body/eval_jaxpr/ppermute | solution.py:20
  880.5 21.8 %collective-permute-done = bf16[2,4,96,256]{2,1,0,3:T(4,128)(2,1)S(1)} collective-permute-done((bf16[2,4,96,256]{2,1,0,3:T(4,128)(2,1)S(1)}, bf16[2,4,96,256]{2,1,0,3:T(4,128)(2,1)S(1)}, u32[]{:S(2)}, u32[]{:S(2)}) %collective-permute-start) | collective-permute-done | bytes 393248 | tf_op jit(solution)/shard_map/while/body/eval_jaxpr/ppermute | solution.py:20
  909.9 20.8 %collective-permute-done = bf16[2,4,96,256]{2,1,0,3:T(4,128)(2,1)S(1)} collective-permute-done((bf16[2,4,96,256]{2,1,0,3:T(4,128)(2,1)S(1)}, bf16[2,4,96,256]{2,1,0,3:T(4,128)(2,1)S(1)}, u32[]{:S(2)}, u32[]{:S(2)}) %collective-permute-start) | collective-permute-done | bytes 393248 | tf_op jit(solution)/shard_map/while/body/eval_jaxpr/ppermute | solution.py:20
  938.3 19.9 %collective-permute-done = bf16[2,4,96,256]{2,1,0,3:T(4,128)(2,1)S(1)} collective-permute-done((bf16[2,4,96,256]{2,1,0,3:T(4,128)(2,1)S(1)}, bf16[2,4,96,256]{2,1,0,3:T(4,128)(2,1)S(1)}, u32[]{:S(2)}, u32[]{:S(2)}) %collective-permute-start) | collective-permute-done | bytes 393248 | tf_op jit(solution)/shard_map/while/body/eval_jaxpr/ppermute | solution.py:20
  965.8 19.0 %collective-permute-done = bf16[2,4,96,256]{2,1,0,3:T(4,128)(2,1)S(1)} collective-permute-done((bf16[2,4,96,256]{2,1,0,3:T(4,128)(2,1)S(1)}, bf16[2,4,96,256]{2,1,0,3:T(4,128)(2,1)S(1)}, u32[]{:S(2)}, u32[]{:S(2)}) %collective-permute-start) | collective-permute-done | bytes 393248 | tf_op jit(solution)/shard_map/while/body/eval_jaxpr/ppermute | solution.py:20
  992.4 17.8 %collective-permute-done = bf16[2,4,96,256]{2,1,0,3:T(4,128)(2,1)S(1)} collective-permute-done((bf16[2,4,96,256]{2,1,0,3:T(4,128)(2,1)S(1)}, bf16[2,4,96,256]{2,1,0,3:T(4,128)(2,1)S(1)}, u32[]{:S(2)}, u32[]{:S(2)}) %collective-permute-start) | collective-permute-done | bytes 393248 | tf_op jit(solution)/shard_map/while/body/eval_jaxpr/ppermute | solution.py:20
  (249 shorter events, 235.8 us)
Async XLA Ops:
  0.0 23.5 %collective-permute-start.1 = (bf16[2,4,24576]{2,1,0:T(4,128)(2,1)}, bf16[2,4,24576]{2,1,0:T(4,128)(2,1)S(1)}, u32[]{:S(2)}, u32[]{:S(2)}) collective-permute-start(bf16[2,4,24576]{2,1,0:T(4,128)(2,1)} %param.3), channel_id=1, source_target_pairs={{0,3},{1,4},{2,5},{3,6},{4,7},{5,8},{6,9},{7,10},{8,11},{9,12},{10... | collective-permute-start | bytes 1179656 | tf_op jit(solution)/shard_map/ppermute | solution.py:15
  2.9 23.0 %collective-permute-start.2 = (bf16[2,4,24576]{2,1,0:T(4,128)(2,1)}, bf16[2,4,24576]{2,1,0:T(4,128)(2,1)S(1)}, u32[]{:S(2)}, u32[]{:S(2)}) collective-permute-start(bf16[2,4,24576]{2,1,0:T(4,128)(2,1)} %param.3), channel_id=1, source_target_pairs={{0,2},{1,3},{2,4},{3,5},{4,6},{5,7},{6,8},{7,9},{8,10},{9,11},{10,... | collective-permute-start | bytes 1179656 | tf_op jit(solution)/shard_map/ppermute | solution.py:15
  6.0 21.8 %collective-permute-start.3 = (bf16[2,4,24576]{2,1,0:T(4,128)(2,1)}, bf16[2,4,24576]{2,1,0:T(4,128)(2,1)S(1)}, u32[]{:S(2)}, u32[]{:S(2)}) collective-permute-start(bf16[2,4,24576]{2,1,0:T(4,128)(2,1)} %param.3), channel_id=1, source_target_pairs={{0,1},{1,2},{2,3},{3,4},{4,5},{5,6},{6,7},{7,8},{8,9},{9,10},{10,1... | collective-permute-start | bytes 1179656 | tf_op jit(solution)/shard_map/ppermute | solution.py:15
  72.3 40.2 %all-to-all-start = ((bf16[16,2,6144]{2,1,0:T(2,128)(2,1)}), bf16[16,2,6144]{2,1,0:T(2,128)(2,1)S(1)}, u32[]{:S(2)}, u32[]{:S(2)}) async-start(bf16[16,2,6144]{2,1,0:T(2,128)(2,1)} %reshape.178), calls=%async_computation | async-start | bytes 786432 | tf_op jit(solution)/shard_map/all_to_all | solution.py:83
  149.0 25.3 %collective-permute-start = (bf16[2,4,96,256]{2,1,0,3:T(4,128)(2,1)S(1)}, bf16[2,4,96,256]{2,1,0,3:T(4,128)(2,1)S(1)}, u32[]{:S(2)}, u32[]{:S(2)}) collective-permute-start(bf16[2,4,96,256]{2,1,0,3:T(4,128)(2,1)S(1)} %get-tuple-element.242), channel_id=1, source_target_pairs={{0,16},{16,32},{32,48},{48,64},{64,80},{80,96},{96,112},{112,128},... | collective-permute-start | bytes 1179656 | tf_op jit(solution)/shard_map/while/body/eval_jaxpr/ppermute | solution.py:20
  180.0 24.2 %collective-permute-start = (bf16[2,4,96,256]{2,1,0,3:T(4,128)(2,1)S(1)}, bf16[2,4,96,256]{2,1,0,3:T(4,128)(2,1)S(1)}, u32[]{:S(2)}, u32[]{:S(2)}) collective-permute-start(bf16[2,4,96,256]{2,1,0,3:T(4,128)(2,1)S(1)} %get-tuple-element.242), channel_id=1, source_target_pairs={{0,16},{16,32},{32,48},{48,64},{64,80},{80,96},{96,112},{112,128},... | collective-permute-start | bytes 1179656 | tf_op jit(solution)/shard_map/while/body/eval_jaxpr/ppermute | solution.py:20
  209.9 23.4 %collective-permute-start = (bf16[2,4,96,256]{2,1,0,3:T(4,128)(2,1)S(1)}, bf16[2,4,96,256]{2,1,0,3:T(4,128)(2,1)S(1)}, u32[]{:S(2)}, u32[]{:S(2)}) collective-permute-start(bf16[2,4,96,256]{2,1,0,3:T(4,128)(2,1)S(1)} %get-tuple-element.242), channel_id=1, source_target_pairs={{0,16},{16,32},{32,48},{48,64},{64,80},{80,96},{96,112},{112,128},... | collective-permute-start | bytes 1179656 | tf_op jit(solution)/shard_map/while/body/eval_jaxpr/ppermute | solution.py:20
  238.9 45.9 %collective-permute-start = (bf16[2,4,96,256]{2,1,0,3:T(4,128)(2,1)S(1)}, bf16[2,4,96,256]{2,1,0,3:T(4,128)(2,1)S(1)}, u32[]{:S(2)}, u32[]{:S(2)}) collective-permute-start(bf16[2,4,96,256]{2,1,0,3:T(4,128)(2,1)S(1)} %get-tuple-element.242), channel_id=1, source_target_pairs={{0,16},{16,32},{32,48},{48,64},{64,80},{80,96},{96,112},{112,128},... | collective-permute-start | bytes 1179656 | tf_op jit(solution)/shard_map/while/body/eval_jaxpr/ppermute | solution.py:20
  290.4 23.0 %collective-permute-start = (bf16[2,4,96,256]{2,1,0,3:T(4,128)(2,1)S(1)}, bf16[2,4,96,256]{2,1,0,3:T(4,128)(2,1)S(1)}, u32[]{:S(2)}, u32[]{:S(2)}) collective-permute-start(bf16[2,4,96,256]{2,1,0,3:T(4,128)(2,1)S(1)} %get-tuple-element.242), channel_id=1, source_target_pairs={{0,16},{16,32},{32,48},{48,64},{64,80},{80,96},{96,112},{112,128},... | collective-permute-start | bytes 1179656 | tf_op jit(solution)/shard_map/while/body/eval_jaxpr/ppermute | solution.py:20
  319.1 22.1 %collective-permute-start = (bf16[2,4,96,256]{2,1,0,3:T(4,128)(2,1)S(1)}, bf16[2,4,96,256]{2,1,0,3:T(4,128)(2,1)S(1)}, u32[]{:S(2)}, u32[]{:S(2)}) collective-permute-start(bf16[2,4,96,256]{2,1,0,3:T(4,128)(2,1)S(1)} %get-tuple-element.242), channel_id=1, source_target_pairs={{0,16},{16,32},{32,48},{48,64},{64,80},{80,96},{96,112},{112,128},... | collective-permute-start | bytes 1179656 | tf_op jit(solution)/shard_map/while/body/eval_jaxpr/ppermute | solution.py:20
  346.8 21.2 %collective-permute-start = (bf16[2,4,96,256]{2,1,0,3:T(4,128)(2,1)S(1)}, bf16[2,4,96,256]{2,1,0,3:T(4,128)(2,1)S(1)}, u32[]{:S(2)}, u32[]{:S(2)}) collective-permute-start(bf16[2,4,96,256]{2,1,0,3:T(4,128)(2,1)S(1)} %get-tuple-element.242), channel_id=1, source_target_pairs={{0,16},{16,32},{32,48},{48,64},{64,80},{80,96},{96,112},{112,128},... | collective-permute-start | bytes 1179656 | tf_op jit(solution)/shard_map/while/body/eval_jaxpr/ppermute | solution.py:20
  373.6 20.2 %collective-permute-start = (bf16[2,4,96,256]{2,1,0,3:T(4,128)(2,1)S(1)}, bf16[2,4,96,256]{2,1,0,3:T(4,128)(2,1)S(1)}, u32[]{:S(2)}, u32[]{:S(2)}) collective-permute-start(bf16[2,4,96,256]{2,1,0,3:T(4,128)(2,1)S(1)} %get-tuple-element.242), channel_id=1, source_target_pairs={{0,16},{16,32},{32,48},{48,64},{64,80},{80,96},{96,112},{112,128},... | collective-permute-start | bytes 1179656 | tf_op jit(solution)/shard_map/while/body/eval_jaxpr/ppermute | solution.py:20
  399.5 19.8 %collective-permute-start = (bf16[2,4,96,256]{2,1,0,3:T(4,128)(2,1)S(1)}, bf16[2,4,96,256]{2,1,0,3:T(4,128)(2,1)S(1)}, u32[]{:S(2)}, u32[]{:S(2)}) collective-permute-start(bf16[2,4,96,256]{2,1,0,3:T(4,128)(2,1)S(1)} %get-tuple-element.242), channel_id=1, source_target_pairs={{0,16},{16,32},{32,48},{48,64},{64,80},{80,96},{96,112},{112,128},... | collective-permute-start | bytes 1179656 | tf_op jit(solution)/shard_map/while/body/eval_jaxpr/ppermute | solution.py:20
  425.0 19.8 %collective-permute-start = (bf16[2,4,96,256]{2,1,0,3:T(4,128)(2,1)S(1)}, bf16[2,4,96,256]{2,1,0,3:T(4,128)(2,1)S(1)}, u32[]{:S(2)}, u32[]{:S(2)}) collective-permute-start(bf16[2,4,96,256]{2,1,0,3:T(4,128)(2,1)S(1)} %get-tuple-element.242), channel_id=1, source_target_pairs={{0,16},{16,32},{32,48},{48,64},{64,80},{80,96},{96,112},{112,128},... | collective-permute-start | bytes 1179656 | tf_op jit(solution)/shard_map/while/body/eval_jaxpr/ppermute | solution.py:20
  450.4 19.8 %collective-permute-start = (bf16[2,4,96,256]{2,1,0,3:T(4,128)(2,1)S(1)}, bf16[2,4,96,256]{2,1,0,3:T(4,128)(2,1)S(1)}, u32[]{:S(2)}, u32[]{:S(2)}) collective-permute-start(bf16[2,4,96,256]{2,1,0,3:T(4,128)(2,1)S(1)} %get-tuple-element.242), channel_id=1, source_target_pairs={{0,16},{16,32},{32,48},{48,64},{64,80},{80,96},{96,112},{112,128},... | collective-permute-start | bytes 1179656 | tf_op jit(solution)/shard_map/while/body/eval_jaxpr/ppermute | solution.py:20
  475.8 19.8 %collective-permute-start = (bf16[2,4,96,256]{2,1,0,3:T(4,128)(2,1)S(1)}, bf16[2,4,96,256]{2,1,0,3:T(4,128)(2,1)S(1)}, u32[]{:S(2)}, u32[]{:S(2)}) collective-permute-start(bf16[2,4,96,256]{2,1,0,3:T(4,128)(2,1)S(1)} %get-tuple-element.242), channel_id=1, source_target_pairs={{0,16},{16,32},{32,48},{48,64},{64,80},{80,96},{96,112},{112,128},... | collective-permute-start | bytes 1179656 | tf_op jit(solution)/shard_map/while/body/eval_jaxpr/ppermute | solution.py:20
  501.3 19.8 %collective-permute-start = (bf16[2,4,96,256]{2,1,0,3:T(4,128)(2,1)S(1)}, bf16[2,4,96,256]{2,1,0,3:T(4,128)(2,1)S(1)}, u32[]{:S(2)}, u32[]{:S(2)}) collective-permute-start(bf16[2,4,96,256]{2,1,0,3:T(4,128)(2,1)S(1)} %get-tuple-element.242), channel_id=1, source_target_pairs={{0,16},{16,32},{32,48},{48,64},{64,80},{80,96},{96,112},{112,128},... | collective-permute-start | bytes 1179656 | tf_op jit(solution)/shard_map/while/body/eval_jaxpr/ppermute | solution.py:20
  526.7 19.8 %collective-permute-start = (bf16[2,4,96,256]{2,1,0,3:T(4,128)(2,1)S(1)}, bf16[2,4,96,256]{2,1,0,3:T(4,128)(2,1)S(1)}, u32[]{:S(2)}, u32[]{:S(2)}) collective-permute-start(bf16[2,4,96,256]{2,1,0,3:T(4,128)(2,1)S(1)} %get-tuple-element.242), channel_id=1, source_target_pairs={{0,16},{16,32},{32,48},{48,64},{64,80},{80,96},{96,112},{112,128},... | collective-permute-start | bytes 1179656 | tf_op jit(solution)/shard_map/while/body/eval_jaxpr/ppermute | solution.py:20
  552.2 19.8 %collective-permute-start = (bf16[2,4,96,256]{2,1,0,3:T(4,128)(2,1)S(1)}, bf16[2,4,96,256]{2,1,0,3:T(4,128)(2,1)S(1)}, u32[]{:S(2)}, u32[]{:S(2)}) collective-permute-start(bf16[2,4,96,256]{2,1,0,3:T(4,128)(2,1)S(1)} %get-tuple-element.242), channel_id=1, source_target_pairs={{0,16},{16,32},{32,48},{48,64},{64,80},{80,96},{96,112},{112,128},... | collective-permute-start | bytes 1179656 | tf_op jit(solution)/shard_map/while/body/eval_jaxpr/ppermute | solution.py:20
  577.6 19.8 %collective-permute-start = (bf16[2,4,96,256]{2,1,0,3:T(4,128)(2,1)S(1)}, bf16[2,4,96,256]{2,1,0,3:T(4,128)(2,1)S(1)}, u32[]{:S(2)}, u32[]{:S(2)}) collective-permute-start(bf16[2,4,96,256]{2,1,0,3:T(4,128)(2,1)S(1)} %get-tuple-element.242), channel_id=1, source_target_pairs={{0,16},{16,32},{32,48},{48,64},{64,80},{80,96},{96,112},{112,128},... | collective-permute-start | bytes 1179656 | tf_op jit(solution)/shard_map/while/body/eval_jaxpr/ppermute | solution.py:20
  603.0 19.8 %collective-permute-start = (bf16[2,4,96,256]{2,1,0,3:T(4,128)(2,1)S(1)}, bf16[2,4,96,256]{2,1,0,3:T(4,128)(2,1)S(1)}, u32[]{:S(2)}, u32[]{:S(2)}) collective-permute-start(bf16[2,4,96,256]{2,1,0,3:T(4,128)(2,1)S(1)} %get-tuple-element.242), channel_id=1, source_target_pairs={{0,16},{16,32},{32,48},{48,64},{64,80},{80,96},{96,112},{112,128},... | collective-permute-start | bytes 1179656 | tf_op jit(solution)/shard_map/while/body/eval_jaxpr/ppermute | solution.py:20
  628.5 19.8 %collective-permute-start = (bf16[2,4,96,256]{2,1,0,3:T(4,128)(2,1)S(1)}, bf16[2,4,96,256]{2,1,0,3:T(4,128)(2,1)S(1)}, u32[]{:S(2)}, u32[]{:S(2)}) collective-permute-start(bf16[2,4,96,256]{2,1,0,3:T(4,128)(2,1)S(1)} %get-tuple-element.242), channel_id=1, source_target_pairs={{0,16},{16,32},{32,48},{48,64},{64,80},{80,96},{96,112},{112,128},... | collective-permute-start | bytes 1179656 | tf_op jit(solution)/shard_map/while/body/eval_jaxpr/ppermute | solution.py:20
  653.9 19.8 %collective-permute-start = (bf16[2,4,96,256]{2,1,0,3:T(4,128)(2,1)S(1)}, bf16[2,4,96,256]{2,1,0,3:T(4,128)(2,1)S(1)}, u32[]{:S(2)}, u32[]{:S(2)}) collective-permute-start(bf16[2,4,96,256]{2,1,0,3:T(4,128)(2,1)S(1)} %get-tuple-element.242), channel_id=1, source_target_pairs={{0,16},{16,32},{32,48},{48,64},{64,80},{80,96},{96,112},{112,128},... | collective-permute-start | bytes 1179656 | tf_op jit(solution)/shard_map/while/body/eval_jaxpr/ppermute | solution.py:20
  679.4 19.8 %collective-permute-start = (bf16[2,4,96,256]{2,1,0,3:T(4,128)(2,1)S(1)}, bf16[2,4,96,256]{2,1,0,3:T(4,128)(2,1)S(1)}, u32[]{:S(2)}, u32[]{:S(2)}) collective-permute-start(bf16[2,4,96,256]{2,1,0,3:T(4,128)(2,1)S(1)} %get-tuple-element.242), channel_id=1, source_target_pairs={{0,16},{16,32},{32,48},{48,64},{64,80},{80,96},{96,112},{112,128},... | collective-permute-start | bytes 1179656 | tf_op jit(solution)/shard_map/while/body/eval_jaxpr/ppermute | solution.py:20
  704.8 20.9 %collective-permute-start = (bf16[2,4,96,256]{2,1,0,3:T(4,128)(2,1)S(1)}, bf16[2,4,96,256]{2,1,0,3:T(4,128)(2,1)S(1)}, u32[]{:S(2)}, u32[]{:S(2)}) collective-permute-start(bf16[2,4,96,256]{2,1,0,3:T(4,128)(2,1)S(1)} %get-tuple-element.242), channel_id=1, source_target_pairs={{0,16},{16,32},{32,48},{48,64},{64,80},{80,96},{96,112},{112,128},... | collective-permute-start | bytes 1179656 | tf_op jit(solution)/shard_map/while/body/eval_jaxpr/ppermute | solution.py:20
  731.3 21.9 %collective-permute-start = (bf16[2,4,96,256]{2,1,0,3:T(4,128)(2,1)S(1)}, bf16[2,4,96,256]{2,1,0,3:T(4,128)(2,1)S(1)}, u32[]{:S(2)}, u32[]{:S(2)}) collective-permute-start(bf16[2,4,96,256]{2,1,0,3:T(4,128)(2,1)S(1)} %get-tuple-element.242), channel_id=1, source_target_pairs={{0,16},{16,32},{32,48},{48,64},{64,80},{80,96},{96,112},{112,128},... | collective-permute-start | bytes 1179656 | tf_op jit(solution)/shard_map/while/body/eval_jaxpr/ppermute | solution.py:20
  758.9 23.0 %collective-permute-start = (bf16[2,4,96,256]{2,1,0,3:T(4,128)(2,1)S(1)}, bf16[2,4,96,256]{2,1,0,3:T(4,128)(2,1)S(1)}, u32[]{:S(2)}, u32[]{:S(2)}) collective-permute-start(bf16[2,4,96,256]{2,1,0,3:T(4,128)(2,1)S(1)} %get-tuple-element.242), channel_id=1, source_target_pairs={{0,16},{16,32},{32,48},{48,64},{64,80},{80,96},{96,112},{112,128},... | collective-permute-start | bytes 1179656 | tf_op jit(solution)/shard_map/while/body/eval_jaxpr/ppermute | solution.py:20
  787.6 24.1 %collective-permute-start = (bf16[2,4,96,256]{2,1,0,3:T(4,128)(2,1)S(1)}, bf16[2,4,96,256]{2,1,0,3:T(4,128)(2,1)S(1)}, u32[]{:S(2)}, u32[]{:S(2)}) collective-permute-start(bf16[2,4,96,256]{2,1,0,3:T(4,128)(2,1)S(1)} %get-tuple-element.242), channel_id=1, source_target_pairs={{0,16},{16,32},{32,48},{48,64},{64,80},{80,96},{96,112},{112,128},... | collective-permute-start | bytes 1179656 | tf_op jit(solution)/shard_map/while/body/eval_jaxpr/ppermute | solution.py:20
  817.4 25.3 %collective-permute-start = (bf16[2,4,96,256]{2,1,0,3:T(4,128)(2,1)S(1)}, bf16[2,4,96,256]{2,1,0,3:T(4,128)(2,1)S(1)}, u32[]{:S(2)}, u32[]{:S(2)}) collective-permute-start(bf16[2,4,96,256]{2,1,0,3:T(4,128)(2,1)S(1)} %get-tuple-element.242), channel_id=1, source_target_pairs={{0,16},{16,32},{32,48},{48,64},{64,80},{80,96},{96,112},{112,128},... | collective-permute-start | bytes 1179656 | tf_op jit(solution)/shard_map/while/body/eval_jaxpr/ppermute | solution.py:20
  848.3 24.6 %collective-permute-start = (bf16[2,4,96,256]{2,1,0,3:T(4,128)(2,1)S(1)}, bf16[2,4,96,256]{2,1,0,3:T(4,128)(2,1)S(1)}, u32[]{:S(2)}, u32[]{:S(2)}) collective-permute-start(bf16[2,4,96,256]{2,1,0,3:T(4,128)(2,1)S(1)} %get-tuple-element.242), channel_id=1, source_target_pairs={{0,16},{16,32},{32,48},{48,64},{64,80},{80,96},{96,112},{112,128},... | collective-permute-start | bytes 1179656 | tf_op jit(solution)/shard_map/while/body/eval_jaxpr/ppermute | solution.py:20
  878.6 23.7 %collective-permute-start = (bf16[2,4,96,256]{2,1,0,3:T(4,128)(2,1)S(1)}, bf16[2,4,96,256]{2,1,0,3:T(4,128)(2,1)S(1)}, u32[]{:S(2)}, u32[]{:S(2)}) collective-permute-start(bf16[2,4,96,256]{2,1,0,3:T(4,128)(2,1)S(1)} %get-tuple-element.242), channel_id=1, source_target_pairs={{0,16},{16,32},{32,48},{48,64},{64,80},{80,96},{96,112},{112,128},... | collective-permute-start | bytes 1179656 | tf_op jit(solution)/shard_map/while/body/eval_jaxpr/ppermute | solution.py:20
  907.9 22.8 %collective-permute-start = (bf16[2,4,96,256]{2,1,0,3:T(4,128)(2,1)S(1)}, bf16[2,4,96,256]{2,1,0,3:T(4,128)(2,1)S(1)}, u32[]{:S(2)}, u32[]{:S(2)}) collective-permute-start(bf16[2,4,96,256]{2,1,0,3:T(4,128)(2,1)S(1)} %get-tuple-element.242), channel_id=1, source_target_pairs={{0,16},{16,32},{32,48},{48,64},{64,80},{80,96},{96,112},{112,128},... | collective-permute-start | bytes 1179656 | tf_op jit(solution)/shard_map/while/body/eval_jaxpr/ppermute | solution.py:20
  936.4 21.9 %collective-permute-start = (bf16[2,4,96,256]{2,1,0,3:T(4,128)(2,1)S(1)}, bf16[2,4,96,256]{2,1,0,3:T(4,128)(2,1)S(1)}, u32[]{:S(2)}, u32[]{:S(2)}) collective-permute-start(bf16[2,4,96,256]{2,1,0,3:T(4,128)(2,1)S(1)} %get-tuple-element.242), channel_id=1, source_target_pairs={{0,16},{16,32},{32,48},{48,64},{64,80},{80,96},{96,112},{112,128},... | collective-permute-start | bytes 1179656 | tf_op jit(solution)/shard_map/while/body/eval_jaxpr/ppermute | solution.py:20
  963.9 21.0 %collective-permute-start = (bf16[2,4,96,256]{2,1,0,3:T(4,128)(2,1)S(1)}, bf16[2,4,96,256]{2,1,0,3:T(4,128)(2,1)S(1)}, u32[]{:S(2)}, u32[]{:S(2)}) collective-permute-start(bf16[2,4,96,256]{2,1,0,3:T(4,128)(2,1)S(1)} %get-tuple-element.242), channel_id=1, source_target_pairs={{0,16},{16,32},{32,48},{48,64},{64,80},{80,96},{96,112},{112,128},... | collective-permute-start | bytes 1179656 | tf_op jit(solution)/shard_map/while/body/eval_jaxpr/ppermute | solution.py:20
  990.5 19.8 %collective-permute-start = (bf16[2,4,96,256]{2,1,0,3:T(4,128)(2,1)S(1)}, bf16[2,4,96,256]{2,1,0,3:T(4,128)(2,1)S(1)}, u32[]{:S(2)}, u32[]{:S(2)}) collective-permute-start(bf16[2,4,96,256]{2,1,0,3:T(4,128)(2,1)S(1)} %get-tuple-element.242), channel_id=1, source_target_pairs={{0,16},{16,32},{32,48},{48,64},{64,80},{80,96},{96,112},{112,128},... | collective-permute-start | bytes 1179656 | tf_op jit(solution)/shard_map/while/body/eval_jaxpr/ppermute | solution.py:20
  1015.9 1.0 copy-start
where the time goes:
time: 1020 us
  waiting for transfers between devices  610 us (60%)
  matrix products  152 us (15%)
  starting transfers between devices  146 us (14%)
  local copies, waits for them, and re-layouts  88 us (9%)
  other arithmetic  18.4 us (2%)
    ppermute x31, waiting for transfers between devices, from_behind(): return lax.ppermute(x, axis, [(i, (i + by) % count) for i in range(count)])  591 us
    dot_general x32, matrix products, correlate(): jnp.einsum('aifc,bjfc->abijc', turned, other, preferred_element_type=jnp....  150 us
    ppermute x31, starting transfers between devices, from_behind(): return lax.ppermute(x, axis, [(i, (i + by) % count) for i in range(count)])  100 us
    unnamed x5, local copies, waits for them, and re-layouts  35.5 us
    all_to_all x1, starting transfers between devices, shards(): lax.all_to_all(spectra, 'tm', split_axis=3, concat_axis=2, tiled=True)  25.2 us
    ppermute x3, starting transfers between devices, passed_along(): lax.ppermute(value, axis, [(source, source + steps) for source in range(l...  20.8 us
  transfers between devices with their start and end apart: 35, of which 34 were waited for; matrix products, arithmetic and copies ran while one was open for 0% of the time, Pallas kernels for 0%

commit v1 on v0

--- a/solution.py
+++ b/solution.py
@@ -80,7 +80,10 @@
     for tap in range(TAPS):
         filtered = filtered + joined[:, :, tap : tap + frames_dev, :] * taps_table[tap]
     spectra = transform(filtered.astype(jnp.bfloat16))
-    turned = lax.all_to_all(spectra, "tm", split_axis=3, concat_axis=2, tiled=True)
+    turned = jnp.concatenate(
+        lax.all_to_all(jnp.stack(jnp.split(spectra, lax.axis_size("tm"), axis=3)), "tm", 0, 0),
+        axis=2,
+    )
     frames_all = turned.shape[2]
     width = turned.shape[3]
     count = lax.axis_size("stn")

time: 1020 us -> 980 us (0.961)
  local copies, waits for them, and re-layouts: 88 us -> 42.3 us
    unnamed x5 -> x20, local copies, waits for them, and re-layouts: 35.5 us -> 11.3 us
    convert_element_type x1 -> x2, local copies, waits for them, and re-layouts: 14.1 us -> 0.9 us  [transform(): return (second / radix).astype(jnp.bfloat16)]
  transfers between devices with their start and end apart: 35 -> 35, of which waited for: 34 -> 33; matrix products, arithmetic and copies ran while one was open for 0% -> 0% of each run, Pallas kernels for 0% -> 0%
where the time goes in v1:
time: 980 us; the launch traced here: 979 us
  waiting for transfers between devices  608 us (62%)
  starting transfers between devices  156 us (16%)
  matrix products  152 us (16%)
  local copies, waits for them, and re-layouts  42.3 us (4%)
  other arithmetic  18.4 us (2%)
    ppermute x31, waiting for transfers between devices, from_behind(): return lax.ppermute(x, axis, [(i, (i + by) % count) for i in range(count)])  589 us
    dot_general x32, matrix products, correlate(): jnp.einsum('aifc,bjfc->abijc', turned, other, preferred_element_type=jnp....  150 us
    ppermute x31, starting transfers between devices, from_behind(): return lax.ppermute(x, axis, [(i, (i + by) % count) for i in range(count)])  104 us
    all_to_all x1, starting transfers between devices, shards(): lax.all_to_all(jnp.stack(jnp.split(spectra, lax.axis_size('tm'), axis=3))...  29.6 us
    ppermute x3, starting transfers between devices, passed_along(): lax.ppermute(value, axis, [(source, source + steps) for source in range(l...  21.6 us
  transfers between devices with their start and end apart: 35, of which 33 were waited for; matrix products, arithmetic and copies ran while one was open for 0% of the time, Pallas kernels for 0%

profile of v1, /device:TPU:2, one launch (start us, length us, event | category | flops | bytes accessed | tf_op | source)
XLA Modules:
  0.0 979.1 jit_solution(12344939698533620577)
XLA Ops:
  5.3 16.3 %collective-permute-start.1 = (bf16[2,4,24576]{2,1,0:T(4,128)(2,1)}, bf16[2,4,24576]{2,1,0:T(4,128)(2,1)S(1)}, u32[]{:S(2)}, u32[]{:S(2)}) collective-permute-start(bf16[2,4,24576]{2,1,0:T(4,128)(2,1)} %param.3), channel_id=1, source_target_pairs={{0,3},{1,4},{2,5},{3,6},{4,7},{5,8},{6,9},{7,10},{8,11},{9,12},{10... | collective-permute-start | bytes 1179656 | tf_op jit(solution)/shard_map/ppermute | solution.py:15
  54.7 29.6 %all-to-all-start = ((bf16[16,2,4,6,256]{4,2,3,1,0:T(4,128)(2,1)}), bf16[16,2,4,6,256]{4,2,3,1,0:T(4,128)(2,1)S(1)}, u32[]{:S(2)}, u32[]{:S(2)}) async-start(bf16[16,2,4,6,256]{4,2,3,1,0:T(4,128)(2,1)} %constant_dynamic-update-slice_fusion), calls=%async_computation | async-start | bytes 786432 | tf_op jit(solution)/shard_map/all_to_all | solution.py:84
  84.3 15.3 %all-to-all-done = bf16[16,2,4,6,256]{4,2,3,1,0:T(4,128)(2,1)S(1)} async-done(((bf16[16,2,4,6,256]{4,2,3,1,0:T(4,128)(2,1)}), bf16[16,2,4,6,256]{4,2,3,1,0:T(4,128)(2,1)S(1)}, u32[]{:S(2)}, u32[]{:S(2)}) %all-to-all-start) | async-done | bytes 393248 | tf_op jit(solution)/shard_map/all_to_all | solution.py:84
  108.1 870.0 %while.17 = (s32[]{:T(128)}, bf16[2,4,96,256]{2,1,0,3:T(4,128)(2,1)S(1)}, f32[2,4,128,256]{3,2,1,0:T(8,128)S(1)}, bf16[2,4,96,256]{2,1,0,3:T(4,128)(2,1)S(1)}, s...) while((s32[]{:T(128)}, ...), condition=%wide.region_1.2_spmd, body=%wide.region_0.1_spmd.sunk | while | flops 3170322 | bytes 3440960 | solution.py:112
  111.6 25.3 %collective-permute-done = bf16[2,4,96,256]{2,1,0,3:T(4,128)(2,1)S(1)} collective-permute-done((bf16[2,4,96,256]{2,1,0,3:T(4,128)(2,1)S(1)}, bf16[2,4,96,256]{2,1,0,3:T(4,128)(2,1)S(1)}, u32[]{:S(2)}, u32[]{:S(2)}) %collective-permute-start) | collective-permute-done | bytes 393248 | tf_op jit(solution)/shard_map/while/body/eval_jaxpr/ppermute | solution.py:20
  136.9 4.7 convolution_bitcast_fusion.3
  144.5 22.5 %collective-permute-done = bf16[2,4,96,256]{2,1,0,3:T(4,128)(2,1)S(1)} collective-permute-done((bf16[2,4,96,256]{2,1,0,3:T(4,128)(2,1)S(1)}, bf16[2,4,96,256]{2,1,0,3:T(4,128)(2,1)S(1)}, u32[]{:S(2)}, u32[]{:S(2)}) %collective-permute-start) | collective-permute-done | bytes 393248 | tf_op jit(solution)/shard_map/while/body/eval_jaxpr/ppermute | solution.py:20
  167.1 4.7 convolution_bitcast_fusion.3
  174.7 21.5 %collective-permute-done = bf16[2,4,96,256]{2,1,0,3:T(4,128)(2,1)S(1)} collective-permute-done((bf16[2,4,96,256]{2,1,0,3:T(4,128)(2,1)S(1)}, bf16[2,4,96,256]{2,1,0,3:T(4,128)(2,1)S(1)}, u32[]{:S(2)}, u32[]{:S(2)}) %collective-permute-start) | collective-permute-done | bytes 393248 | tf_op jit(solution)/shard_map/while/body/eval_jaxpr/ppermute | solution.py:20
  196.2 4.7 convolution_bitcast_fusion.3
  201.8 40.7 %collective-permute-start = (bf16[2,4,96,256]{2,1,0,3:T(4,128)(2,1)S(1)}, bf16[2,4,96,256]{2,1,0,3:T(4,128)(2,1)S(1)}, u32[]{:S(2)}, u32[]{:S(2)}) collective-permute-start(bf16[2,4,96,256]{2,1,0,3:T(4,128)(2,1)S(1)} %get-tuple-element.237), channel_id=1, source_target_pairs={{0,16},{16,32},{32,48},{48,64},{64,80},{80,96},{96,112},{112,128},... | collective-permute-start | bytes 1179656 | tf_op jit(solution)/shard_map/while/body/eval_jaxpr/ppermute | solution.py:20
  242.5 9.4 collective-permute-done
  257.6 6.5 collective-permute-start
  264.1 15.1 %collective-permute-done = bf16[2,4,96,256]{2,1,0,3:T(4,128)(2,1)S(1)} collective-permute-done((bf16[2,4,96,256]{2,1,0,3:T(4,128)(2,1)S(1)}, bf16[2,4,96,256]{2,1,0,3:T(4,128)(2,1)S(1)}, u32[]{:S(2)}, u32[]{:S(2)}) %collective-permute-start) | collective-permute-done | bytes 393248 | tf_op jit(solution)/shard_map/while/body/eval_jaxpr/ppermute | solution.py:20
  279.3 4.7 convolution_bitcast_fusion.3
  286.9 18.8 %collective-permute-done = bf16[2,4,96,256]{2,1,0,3:T(4,128)(2,1)S(1)} collective-permute-done((bf16[2,4,96,256]{2,1,0,3:T(4,128)(2,1)S(1)}, bf16[2,4,96,256]{2,1,0,3:T(4,128)(2,1)S(1)}, u32[]{:S(2)}, u32[]{:S(2)}) %collective-permute-start) | collective-permute-done | bytes 393248 | tf_op jit(solution)/shard_map/while/body/eval_jaxpr/ppermute | solution.py:20
  305.6 4.7 convolution_bitcast_fusion.3
  313.2 17.8 %collective-permute-done = bf16[2,4,96,256]{2,1,0,3:T(4,128)(2,1)S(1)} collective-permute-done((bf16[2,4,96,256]{2,1,0,3:T(4,128)(2,1)S(1)}, bf16[2,4,96,256]{2,1,0,3:T(4,128)(2,1)S(1)}, u32[]{:S(2)}, u32[]{:S(2)}) %collective-permute-start) | collective-permute-done | bytes 393248 | tf_op jit(solution)/shard_map/while/body/eval_jaxpr/ppermute | solution.py:20
  331.1 4.7 convolution_bitcast_fusion.3
  338.7 17.8 %collective-permute-done = bf16[2,4,96,256]{2,1,0,3:T(4,128)(2,1)S(1)} collective-permute-done((bf16[2,4,96,256]{2,1,0,3:T(4,128)(2,1)S(1)}, bf16[2,4,96,256]{2,1,0,3:T(4,128)(2,1)S(1)}, u32[]{:S(2)}, u32[]{:S(2)}) %collective-permute-start) | collective-permute-done | bytes 393248 | tf_op jit(solution)/shard_map/while/body/eval_jaxpr/ppermute | solution.py:20
  356.5 4.7 convolution_bitcast_fusion.3
  364.1 17.8 %collective-permute-done = bf16[2,4,96,256]{2,1,0,3:T(4,128)(2,1)S(1)} collective-permute-done((bf16[2,4,96,256]{2,1,0,3:T(4,128)(2,1)S(1)}, bf16[2,4,96,256]{2,1,0,3:T(4,128)(2,1)S(1)}, u32[]{:S(2)}, u32[]{:S(2)}) %collective-permute-start) | collective-permute-done | bytes 393248 | tf_op jit(solution)/shard_map/while/body/eval_jaxpr/ppermute | solution.py:20
  382.0 4.7 convolution_bitcast_fusion.3
  389.6 17.8 %collective-permute-done = bf16[2,4,96,256]{2,1,0,3:T(4,128)(2,1)S(1)} collective-permute-done((bf16[2,4,96,256]{2,1,0,3:T(4,128)(2,1)S(1)}, bf16[2,4,96,256]{2,1,0,3:T(4,128)(2,1)S(1)}, u32[]{:S(2)}, u32[]{:S(2)}) %collective-permute-start) | collective-permute-done | bytes 393248 | tf_op jit(solution)/shard_map/while/body/eval_jaxpr/ppermute | solution.py:20
  407.4 4.7 convolution_bitcast_fusion.3
  415.0 17.8 %collective-permute-done = bf16[2,4,96,256]{2,1,0,3:T(4,128)(2,1)S(1)} collective-permute-done((bf16[2,4,96,256]{2,1,0,3:T(4,128)(2,1)S(1)}, bf16[2,4,96,256]{2,1,0,3:T(4,128)(2,1)S(1)}, u32[]{:S(2)}, u32[]{:S(2)}) %collective-permute-start) | collective-permute-done | bytes 393248 | tf_op jit(solution)/shard_map/while/body/eval_jaxpr/ppermute | solution.py:20
  432.8 4.7 convolution_bitcast_fusion.3
  440.4 17.8 %collective-permute-done = bf16[2,4,96,256]{2,1,0,3:T(4,128)(2,1)S(1)} collective-permute-done((bf16[2,4,96,256]{2,1,0,3:T(4,128)(2,1)S(1)}, bf16[2,4,96,256]{2,1,0,3:T(4,128)(2,1)S(1)}, u32[]{:S(2)}, u32[]{:S(2)}) %collective-permute-start) | collective-permute-done | bytes 393248 | tf_op jit(solution)/shard_map/while/body/eval_jaxpr/ppermute | solution.py:20
  458.3 4.7 convolution_bitcast_fusion.3
  465.9 17.8 %collective-permute-done = bf16[2,4,96,256]{2,1,0,3:T(4,128)(2,1)S(1)} collective-permute-done((bf16[2,4,96,256]{2,1,0,3:T(4,128)(2,1)S(1)}, bf16[2,4,96,256]{2,1,0,3:T(4,128)(2,1)S(1)}, u32[]{:S(2)}, u32[]{:S(2)}) %collective-permute-start) | collective-permute-done | bytes 393248 | tf_op jit(solution)/shard_map/while/body/eval_jaxpr/ppermute | solution.py:20
  491.3 17.8 %collective-permute-done = bf16[2,4,96,256]{2,1,0,3:T(4,128)(2,1)S(1)} collective-permute-done((bf16[2,4,96,256]{2,1,0,3:T(4,128)(2,1)S(1)}, bf16[2,4,96,256]{2,1,0,3:T(4,128)(2,1)S(1)}, u32[]{:S(2)}, u32[]{:S(2)}) %collective-permute-start) | collective-permute-done | bytes 393248 | tf_op jit(solution)/shard_map/while/body/eval_jaxpr/ppermute | solution.py:20
  516.8 17.8 %collective-permute-done = bf16[2,4,96,256]{2,1,0,3:T(4,128)(2,1)S(1)} collective-permute-done((bf16[2,4,96,256]{2,1,0,3:T(4,128)(2,1)S(1)}, bf16[2,4,96,256]{2,1,0,3:T(4,128)(2,1)S(1)}, u32[]{:S(2)}, u32[]{:S(2)}) %collective-permute-start) | collective-permute-done | bytes 393248 | tf_op jit(solution)/shard_map/while/body/eval_jaxpr/ppermute | solution.py:20
  542.2 17.8 %collective-permute-done = bf16[2,4,96,256]{2,1,0,3:T(4,128)(2,1)S(1)} collective-permute-done((bf16[2,4,96,256]{2,1,0,3:T(4,128)(2,1)S(1)}, bf16[2,4,96,256]{2,1,0,3:T(4,128)(2,1)S(1)}, u32[]{:S(2)}, u32[]{:S(2)}) %collective-permute-start) | collective-permute-done | bytes 393248 | tf_op jit(solution)/shard_map/while/body/eval_jaxpr/ppermute | solution.py:20
  567.6 17.8 %collective-permute-done = bf16[2,4,96,256]{2,1,0,3:T(4,128)(2,1)S(1)} collective-permute-done((bf16[2,4,96,256]{2,1,0,3:T(4,128)(2,1)S(1)}, bf16[2,4,96,256]{2,1,0,3:T(4,128)(2,1)S(1)}, u32[]{:S(2)}, u32[]{:S(2)}) %collective-permute-start) | collective-permute-done | bytes 393248 | tf_op jit(solution)/shard_map/while/body/eval_jaxpr/ppermute | solution.py:20
  593.1 17.8 %collective-permute-done = bf16[2,4,96,256]{2,1,0,3:T(4,128)(2,1)S(1)} collective-permute-done((bf16[2,4,96,256]{2,1,0,3:T(4,128)(2,1)S(1)}, bf16[2,4,96,256]{2,1,0,3:T(4,128)(2,1)S(1)}, u32[]{:S(2)}, u32[]{:S(2)}) %collective-permute-start) | collective-permute-done | bytes 393248 | tf_op jit(solution)/shard_map/while/body/eval_jaxpr/ppermute | solution.py:20
  618.5 18.5 %collective-permute-done = bf16[2,4,96,256]{2,1,0,3:T(4,128)(2,1)S(1)} collective-permute-done((bf16[2,4,96,256]{2,1,0,3:T(4,128)(2,1)S(1)}, bf16[2,4,96,256]{2,1,0,3:T(4,128)(2,1)S(1)}, u32[]{:S(2)}, u32[]{:S(2)}) %collective-permute-start) | collective-permute-done | bytes 393248 | tf_op jit(solution)/shard_map/while/body/eval_jaxpr/ppermute | solution.py:20
  644.6 19.6 %collective-permute-done = bf16[2,4,96,256]{2,1,0,3:T(4,128)(2,1)S(1)} collective-permute-done((bf16[2,4,96,256]{2,1,0,3:T(4,128)(2,1)S(1)}, bf16[2,4,96,256]{2,1,0,3:T(4,128)(2,1)S(1)}, u32[]{:S(2)}, u32[]{:S(2)}) %collective-permute-start) | collective-permute-done | bytes 393248 | tf_op jit(solution)/shard_map/while/body/eval_jaxpr/ppermute | solution.py:20
  671.8 20.7 %collective-permute-done = bf16[2,4,96,256]{2,1,0,3:T(4,128)(2,1)S(1)} collective-permute-done((bf16[2,4,96,256]{2,1,0,3:T(4,128)(2,1)S(1)}, bf16[2,4,96,256]{2,1,0,3:T(4,128)(2,1)S(1)}, u32[]{:S(2)}, u32[]{:S(2)}) %collective-permute-start) | collective-permute-done | bytes 393248 | tf_op jit(solution)/shard_map/while/body/eval_jaxpr/ppermute | solution.py:20
  700.1 21.7 %collective-permute-done = bf16[2,4,96,256]{2,1,0,3:T(4,128)(2,1)S(1)} collective-permute-done((bf16[2,4,96,256]{2,1,0,3:T(4,128)(2,1)S(1)}, bf16[2,4,96,256]{2,1,0,3:T(4,128)(2,1)S(1)}, u32[]{:S(2)}, u32[]{:S(2)}) %collective-permute-start) | collective-permute-done | bytes 393248 | tf_op jit(solution)/shard_map/while/body/eval_jaxpr/ppermute | solution.py:20
  729.4 23.0 %collective-permute-done = bf16[2,4,96,256]{2,1,0,3:T(4,128)(2,1)S(1)} collective-permute-done((bf16[2,4,96,256]{2,1,0,3:T(4,128)(2,1)S(1)}, bf16[2,4,96,256]{2,1,0,3:T(4,128)(2,1)S(1)}, u32[]{:S(2)}, u32[]{:S(2)}) %collective-permute-start) | collective-permute-done | bytes 393248 | tf_op jit(solution)/shard_map/while/body/eval_jaxpr/ppermute | solution.py:20
  760.0 22.8 %collective-permute-done = bf16[2,4,96,256]{2,1,0,3:T(4,128)(2,1)S(1)} collective-permute-done((bf16[2,4,96,256]{2,1,0,3:T(4,128)(2,1)S(1)}, bf16[2,4,96,256]{2,1,0,3:T(4,128)(2,1)S(1)}, u32[]{:S(2)}, u32[]{:S(2)}) %collective-permute-start) | collective-permute-done | bytes 393248 | tf_op jit(solution)/shard_map/while/body/eval_jaxpr/ppermute | solution.py:20
  790.4 22.0 %collective-permute-done = bf16[2,4,96,256]{2,1,0,3:T(4,128)(2,1)S(1)} collective-permute-done((bf16[2,4,96,256]{2,1,0,3:T(4,128)(2,1)S(1)}, bf16[2,4,96,256]{2,1,0,3:T(4,128)(2,1)S(1)}, u32[]{:S(2)}, u32[]{:S(2)}) %collective-permute-start) | collective-permute-done | bytes 393248 | tf_op jit(solution)/shard_map/while/body/eval_jaxpr/ppermute | solution.py:20
  820.0 21.1 %collective-permute-done = bf16[2,4,96,256]{2,1,0,3:T(4,128)(2,1)S(1)} collective-permute-done((bf16[2,4,96,256]{2,1,0,3:T(4,128)(2,1)S(1)}, bf16[2,4,96,256]{2,1,0,3:T(4,128)(2,1)S(1)}, u32[]{:S(2)}, u32[]{:S(2)}) %collective-permute-start) | collective-permute-done | bytes 393248 | tf_op jit(solution)/shard_map/while/body/eval_jaxpr/ppermute | solution.py:20
  848.7 20.2 %collective-permute-done = bf16[2,4,96,256]{2,1,0,3:T(4,128)(2,1)S(1)} collective-permute-done((bf16[2,4,96,256]{2,1,0,3:T(4,128)(2,1)S(1)}, bf16[2,4,96,256]{2,1,0,3:T(4,128)(2,1)S(1)}, u32[]{:S(2)}, u32[]{:S(2)}) %collective-permute-start) | collective-permute-done | bytes 393248 | tf_op jit(solution)/shard_map/while/body/eval_jaxpr/ppermute | solution.py:20
  876.4 19.2 %collective-permute-done = bf16[2,4,96,256]{2,1,0,3:T(4,128)(2,1)S(1)} collective-permute-done((bf16[2,4,96,256]{2,1,0,3:T(4,128)(2,1)S(1)}, bf16[2,4,96,256]{2,1,0,3:T(4,128)(2,1)S(1)}, u32[]{:S(2)}, u32[]{:S(2)}) %collective-permute-start) | collective-permute-done | bytes 393248 | tf_op jit(solution)/shard_map/while/body/eval_jaxpr/ppermute | solution.py:20
  903.3 18.3 %collective-permute-done = bf16[2,4,96,256]{2,1,0,3:T(4,128)(2,1)S(1)} collective-permute-done((bf16[2,4,96,256]{2,1,0,3:T(4,128)(2,1)S(1)}, bf16[2,4,96,256]{2,1,0,3:T(4,128)(2,1)S(1)}, u32[]{:S(2)}, u32[]{:S(2)}) %collective-permute-start) | collective-permute-done | bytes 393248 | tf_op jit(solution)/shard_map/while/body/eval_jaxpr/ppermute | solution.py:20
  929.2 17.8 %collective-permute-done = bf16[2,4,96,256]{2,1,0,3:T(4,128)(2,1)S(1)} collective-permute-done((bf16[2,4,96,256]{2,1,0,3:T(4,128)(2,1)S(1)}, bf16[2,4,96,256]{2,1,0,3:T(4,128)(2,1)S(1)}, u32[]{:S(2)}, u32[]{:S(2)}) %collective-permute-start) | collective-permute-done | bytes 393248 | tf_op jit(solution)/shard_map/while/body/eval_jaxpr/ppermute | solution.py:20
  954.6 17.8 %collective-permute-done = bf16[2,4,96,256]{2,1,0,3:T(4,128)(2,1)S(1)} collective-permute-done((bf16[2,4,96,256]{2,1,0,3:T(4,128)(2,1)S(1)}, bf16[2,4,96,256]{2,1,0,3:T(4,128)(2,1)S(1)}, u32[]{:S(2)}, u32[]{:S(2)}) %collective-permute-start) | collective-permute-done | bytes 393248 | tf_op jit(solution)/shard_map/while/body/eval_jaxpr/ppermute | solution.py:20
  (265 shorter events, 227.3 us)
Async XLA Ops:
  0.0 24.3 %collective-permute-start.3 = (bf16[2,4,24576]{2,1,0:T(4,128)(2,1)}, bf16[2,4,24576]{2,1,0:T(4,128)(2,1)S(1)}, u32[]{:S(2)}, u32[]{:S(2)}) collective-permute-start(bf16[2,4,24576]{2,1,0:T(4,128)(2,1)} %param.3), channel_id=1, source_target_pairs={{0,1},{1,2},{2,3},{3,4},{4,5},{5,6},{6,7},{7,8},{8,9},{9,10},{10,1... | collective-permute-start | bytes 1179656 | tf_op jit(solution)/shard_map/ppermute | solution.py:15
  1.9 22.4 %collective-permute-start.2 = (bf16[2,4,24576]{2,1,0:T(4,128)(2,1)}, bf16[2,4,24576]{2,1,0:T(4,128)(2,1)S(1)}, u32[]{:S(2)}, u32[]{:S(2)}) collective-permute-start(bf16[2,4,24576]{2,1,0:T(4,128)(2,1)} %param.3), channel_id=1, source_target_pairs={{0,2},{1,3},{2,4},{3,5},{4,6},{5,7},{6,8},{7,9},{8,10},{9,11},{10,... | collective-permute-start | bytes 1179656 | tf_op jit(solution)/shard_map/ppermute | solution.py:15
  5.3 22.5 %collective-permute-start.1 = (bf16[2,4,24576]{2,1,0:T(4,128)(2,1)}, bf16[2,4,24576]{2,1,0:T(4,128)(2,1)S(1)}, u32[]{:S(2)}, u32[]{:S(2)}) collective-permute-start(bf16[2,4,24576]{2,1,0:T(4,128)(2,1)} %param.3), channel_id=1, source_target_pairs={{0,3},{1,4},{2,5},{3,6},{4,7},{5,8},{6,9},{7,10},{8,11},{9,12},{10... | collective-permute-start | bytes 1179656 | tf_op jit(solution)/shard_map/ppermute | solution.py:15
  54.7 44.9 %all-to-all-start = ((bf16[16,2,4,6,256]{4,2,3,1,0:T(4,128)(2,1)}), bf16[16,2,4,6,256]{4,2,3,1,0:T(4,128)(2,1)S(1)}, u32[]{:S(2)}, u32[]{:S(2)}) async-start(bf16[16,2,4,6,256]{4,2,3,1,0:T(4,128)(2,1)} %constant_dynamic-update-slice_fusion), calls=%async_computation | async-start | bytes 786432 | tf_op jit(solution)/shard_map/all_to_all | solution.py:84
  107.0 1.1 copy-start.1
  108.1 28.8 %collective-permute-start = (bf16[2,4,96,256]{2,1,0,3:T(4,128)(2,1)S(1)}, bf16[2,4,96,256]{2,1,0,3:T(4,128)(2,1)S(1)}, u32[]{:S(2)}, u32[]{:S(2)}) collective-permute-start(bf16[2,4,96,256]{2,1,0,3:T(4,128)(2,1)S(1)} %get-tuple-element.237), channel_id=1, source_target_pairs={{0,16},{16,32},{32,48},{48,64},{64,80},{80,96},{96,112},{112,128},... | collective-permute-start | bytes 1179656 | tf_op jit(solution)/shard_map/while/body/eval_jaxpr/ppermute | solution.py:20
  142.6 24.5 %collective-permute-start = (bf16[2,4,96,256]{2,1,0,3:T(4,128)(2,1)S(1)}, bf16[2,4,96,256]{2,1,0,3:T(4,128)(2,1)S(1)}, u32[]{:S(2)}, u32[]{:S(2)}) collective-permute-start(bf16[2,4,96,256]{2,1,0,3:T(4,128)(2,1)S(1)} %get-tuple-element.237), channel_id=1, source_target_pairs={{0,16},{16,32},{32,48},{48,64},{64,80},{80,96},{96,112},{112,128},... | collective-permute-start | bytes 1179656 | tf_op jit(solution)/shard_map/while/body/eval_jaxpr/ppermute | solution.py:20
  172.7 23.4 %collective-permute-start = (bf16[2,4,96,256]{2,1,0,3:T(4,128)(2,1)S(1)}, bf16[2,4,96,256]{2,1,0,3:T(4,128)(2,1)S(1)}, u32[]{:S(2)}, u32[]{:S(2)}) collective-permute-start(bf16[2,4,96,256]{2,1,0,3:T(4,128)(2,1)S(1)} %get-tuple-element.237), channel_id=1, source_target_pairs={{0,16},{16,32},{32,48},{48,64},{64,80},{80,96},{96,112},{112,128},... | collective-permute-start | bytes 1179656 | tf_op jit(solution)/shard_map/while/body/eval_jaxpr/ppermute | solution.py:20
  201.8 50.2 %collective-permute-start = (bf16[2,4,96,256]{2,1,0,3:T(4,128)(2,1)S(1)}, bf16[2,4,96,256]{2,1,0,3:T(4,128)(2,1)S(1)}, u32[]{:S(2)}, u32[]{:S(2)}) collective-permute-start(bf16[2,4,96,256]{2,1,0,3:T(4,128)(2,1)S(1)} %get-tuple-element.237), channel_id=1, source_target_pairs={{0,16},{16,32},{32,48},{48,64},{64,80},{80,96},{96,112},{112,128},... | collective-permute-start | bytes 1179656 | tf_op jit(solution)/shard_map/while/body/eval_jaxpr/ppermute | solution.py:20
  257.6 21.6 %collective-permute-start = (bf16[2,4,96,256]{2,1,0,3:T(4,128)(2,1)S(1)}, bf16[2,4,96,256]{2,1,0,3:T(4,128)(2,1)S(1)}, u32[]{:S(2)}, u32[]{:S(2)}) collective-permute-start(bf16[2,4,96,256]{2,1,0,3:T(4,128)(2,1)S(1)} %get-tuple-element.237), channel_id=1, source_target_pairs={{0,16},{16,32},{32,48},{48,64},{64,80},{80,96},{96,112},{112,128},... | collective-permute-start | bytes 1179656 | tf_op jit(solution)/shard_map/while/body/eval_jaxpr/ppermute | solution.py:20
  284.9 20.7 %collective-permute-start = (bf16[2,4,96,256]{2,1,0,3:T(4,128)(2,1)S(1)}, bf16[2,4,96,256]{2,1,0,3:T(4,128)(2,1)S(1)}, u32[]{:S(2)}, u32[]{:S(2)}) collective-permute-start(bf16[2,4,96,256]{2,1,0,3:T(4,128)(2,1)S(1)} %get-tuple-element.237), channel_id=1, source_target_pairs={{0,16},{16,32},{32,48},{48,64},{64,80},{80,96},{96,112},{112,128},... | collective-permute-start | bytes 1179656 | tf_op jit(solution)/shard_map/while/body/eval_jaxpr/ppermute | solution.py:20
  311.3 19.8 %collective-permute-start = (bf16[2,4,96,256]{2,1,0,3:T(4,128)(2,1)S(1)}, bf16[2,4,96,256]{2,1,0,3:T(4,128)(2,1)S(1)}, u32[]{:S(2)}, u32[]{:S(2)}) collective-permute-start(bf16[2,4,96,256]{2,1,0,3:T(4,128)(2,1)S(1)} %get-tuple-element.237), channel_id=1, source_target_pairs={{0,16},{16,32},{32,48},{48,64},{64,80},{80,96},{96,112},{112,128},... | collective-permute-start | bytes 1179656 | tf_op jit(solution)/shard_map/while/body/eval_jaxpr/ppermute | solution.py:20
  336.7 19.8 %collective-permute-start = (bf16[2,4,96,256]{2,1,0,3:T(4,128)(2,1)S(1)}, bf16[2,4,96,256]{2,1,0,3:T(4,128)(2,1)S(1)}, u32[]{:S(2)}, u32[]{:S(2)}) collective-permute-start(bf16[2,4,96,256]{2,1,0,3:T(4,128)(2,1)S(1)} %get-tuple-element.237), channel_id=1, source_target_pairs={{0,16},{16,32},{32,48},{48,64},{64,80},{80,96},{96,112},{112,128},... | collective-permute-start | bytes 1179656 | tf_op jit(solution)/shard_map/while/body/eval_jaxpr/ppermute | solution.py:20
  362.2 19.8 %collective-permute-start = (bf16[2,4,96,256]{2,1,0,3:T(4,128)(2,1)S(1)}, bf16[2,4,96,256]{2,1,0,3:T(4,128)(2,1)S(1)}, u32[]{:S(2)}, u32[]{:S(2)}) collective-permute-start(bf16[2,4,96,256]{2,1,0,3:T(4,128)(2,1)S(1)} %get-tuple-element.237), channel_id=1, source_target_pairs={{0,16},{16,32},{32,48},{48,64},{64,80},{80,96},{96,112},{112,128},... | collective-permute-start | bytes 1179656 | tf_op jit(solution)/shard_map/while/body/eval_jaxpr/ppermute | solution.py:20
  387.6 19.8 %collective-permute-start = (bf16[2,4,96,256]{2,1,0,3:T(4,128)(2,1)S(1)}, bf16[2,4,96,256]{2,1,0,3:T(4,128)(2,1)S(1)}, u32[]{:S(2)}, u32[]{:S(2)}) collective-permute-start(bf16[2,4,96,256]{2,1,0,3:T(4,128)(2,1)S(1)} %get-tuple-element.237), channel_id=1, source_target_pairs={{0,16},{16,32},{32,48},{48,64},{64,80},{80,96},{96,112},{112,128},... | collective-permute-start | bytes 1179656 | tf_op jit(solution)/shard_map/while/body/eval_jaxpr/ppermute | solution.py:20
  413.1 19.8 %collective-permute-start = (bf16[2,4,96,256]{2,1,0,3:T(4,128)(2,1)S(1)}, bf16[2,4,96,256]{2,1,0,3:T(4,128)(2,1)S(1)}, u32[]{:S(2)}, u32[]{:S(2)}) collective-permute-start(bf16[2,4,96,256]{2,1,0,3:T(4,128)(2,1)S(1)} %get-tuple-element.237), channel_id=1, source_target_pairs={{0,16},{16,32},{32,48},{48,64},{64,80},{80,96},{96,112},{112,128},... | collective-permute-start | bytes 1179656 | tf_op jit(solution)/shard_map/while/body/eval_jaxpr/ppermute | solution.py:20
  438.5 19.8 %collective-permute-start = (bf16[2,4,96,256]{2,1,0,3:T(4,128)(2,1)S(1)}, bf16[2,4,96,256]{2,1,0,3:T(4,128)(2,1)S(1)}, u32[]{:S(2)}, u32[]{:S(2)}) collective-permute-start(bf16[2,4,96,256]{2,1,0,3:T(4,128)(2,1)S(1)} %get-tuple-element.237), channel_id=1, source_target_pairs={{0,16},{16,32},{32,48},{48,64},{64,80},{80,96},{96,112},{112,128},... | collective-permute-start | bytes 1179656 | tf_op jit(solution)/shard_map/while/body/eval_jaxpr/ppermute | solution.py:20
  463.9 19.8 %collective-permute-start = (bf16[2,4,96,256]{2,1,0,3:T(4,128)(2,1)S(1)}, bf16[2,4,96,256]{2,1,0,3:T(4,128)(2,1)S(1)}, u32[]{:S(2)}, u32[]{:S(2)}) collective-permute-start(bf16[2,4,96,256]{2,1,0,3:T(4,128)(2,1)S(1)} %get-tuple-element.237), channel_id=1, source_target_pairs={{0,16},{16,32},{32,48},{48,64},{64,80},{80,96},{96,112},{112,128},... | collective-permute-start | bytes 1179656 | tf_op jit(solution)/shard_map/while/body/eval_jaxpr/ppermute | solution.py:20
  489.4 19.8 %collective-permute-start = (bf16[2,4,96,256]{2,1,0,3:T(4,128)(2,1)S(1)}, bf16[2,4,96,256]{2,1,0,3:T(4,128)(2,1)S(1)}, u32[]{:S(2)}, u32[]{:S(2)}) collective-permute-start(bf16[2,4,96,256]{2,1,0,3:T(4,128)(2,1)S(1)} %get-tuple-element.237), channel_id=1, source_target_pairs={{0,16},{16,32},{32,48},{48,64},{64,80},{80,96},{96,112},{112,128},... | collective-permute-start | bytes 1179656 | tf_op jit(solution)/shard_map/while/body/eval_jaxpr/ppermute | solution.py:20
  514.8 19.8 %collective-permute-start = (bf16[2,4,96,256]{2,1,0,3:T(4,128)(2,1)S(1)}, bf16[2,4,96,256]{2,1,0,3:T(4,128)(2,1)S(1)}, u32[]{:S(2)}, u32[]{:S(2)}) collective-permute-start(bf16[2,4,96,256]{2,1,0,3:T(4,128)(2,1)S(1)} %get-tuple-element.237), channel_id=1, source_target_pairs={{0,16},{16,32},{32,48},{48,64},{64,80},{80,96},{96,112},{112,128},... | collective-permute-start | bytes 1179656 | tf_op jit(solution)/shard_map/while/body/eval_jaxpr/ppermute | solution.py:20
  540.2 19.8 %collective-permute-start = (bf16[2,4,96,256]{2,1,0,3:T(4,128)(2,1)S(1)}, bf16[2,4,96,256]{2,1,0,3:T(4,128)(2,1)S(1)}, u32[]{:S(2)}, u32[]{:S(2)}) collective-permute-start(bf16[2,4,96,256]{2,1,0,3:T(4,128)(2,1)S(1)} %get-tuple-element.237), channel_id=1, source_target_pairs={{0,16},{16,32},{32,48},{48,64},{64,80},{80,96},{96,112},{112,128},... | collective-permute-start | bytes 1179656 | tf_op jit(solution)/shard_map/while/body/eval_jaxpr/ppermute | solution.py:20
  565.7 19.8 %collective-permute-start = (bf16[2,4,96,256]{2,1,0,3:T(4,128)(2,1)S(1)}, bf16[2,4,96,256]{2,1,0,3:T(4,128)(2,1)S(1)}, u32[]{:S(2)}, u32[]{:S(2)}) collective-permute-start(bf16[2,4,96,256]{2,1,0,3:T(4,128)(2,1)S(1)} %get-tuple-element.237), channel_id=1, source_target_pairs={{0,16},{16,32},{32,48},{48,64},{64,80},{80,96},{96,112},{112,128},... | collective-permute-start | bytes 1179656 | tf_op jit(solution)/shard_map/while/body/eval_jaxpr/ppermute | solution.py:20
  591.1 19.8 %collective-permute-start = (bf16[2,4,96,256]{2,1,0,3:T(4,128)(2,1)S(1)}, bf16[2,4,96,256]{2,1,0,3:T(4,128)(2,1)S(1)}, u32[]{:S(2)}, u32[]{:S(2)}) collective-permute-start(bf16[2,4,96,256]{2,1,0,3:T(4,128)(2,1)S(1)} %get-tuple-element.237), channel_id=1, source_target_pairs={{0,16},{16,32},{32,48},{48,64},{64,80},{80,96},{96,112},{112,128},... | collective-permute-start | bytes 1179656 | tf_op jit(solution)/shard_map/while/body/eval_jaxpr/ppermute | solution.py:20
  616.6 20.5 %collective-permute-start = (bf16[2,4,96,256]{2,1,0,3:T(4,128)(2,1)S(1)}, bf16[2,4,96,256]{2,1,0,3:T(4,128)(2,1)S(1)}, u32[]{:S(2)}, u32[]{:S(2)}) collective-permute-start(bf16[2,4,96,256]{2,1,0,3:T(4,128)(2,1)S(1)} %get-tuple-element.237), channel_id=1, source_target_pairs={{0,16},{16,32},{32,48},{48,64},{64,80},{80,96},{96,112},{112,128},... | collective-permute-start | bytes 1179656 | tf_op jit(solution)/shard_map/while/body/eval_jaxpr/ppermute | solution.py:20
  642.7 21.5 %collective-permute-start = (bf16[2,4,96,256]{2,1,0,3:T(4,128)(2,1)S(1)}, bf16[2,4,96,256]{2,1,0,3:T(4,128)(2,1)S(1)}, u32[]{:S(2)}, u32[]{:S(2)}) collective-permute-start(bf16[2,4,96,256]{2,1,0,3:T(4,128)(2,1)S(1)} %get-tuple-element.237), channel_id=1, source_target_pairs={{0,16},{16,32},{32,48},{48,64},{64,80},{80,96},{96,112},{112,128},... | collective-permute-start | bytes 1179656 | tf_op jit(solution)/shard_map/while/body/eval_jaxpr/ppermute | solution.py:20
  669.9 22.6 %collective-permute-start = (bf16[2,4,96,256]{2,1,0,3:T(4,128)(2,1)S(1)}, bf16[2,4,96,256]{2,1,0,3:T(4,128)(2,1)S(1)}, u32[]{:S(2)}, u32[]{:S(2)}) collective-permute-start(bf16[2,4,96,256]{2,1,0,3:T(4,128)(2,1)S(1)} %get-tuple-element.237), channel_id=1, source_target_pairs={{0,16},{16,32},{32,48},{48,64},{64,80},{80,96},{96,112},{112,128},... | collective-permute-start | bytes 1179656 | tf_op jit(solution)/shard_map/while/body/eval_jaxpr/ppermute | solution.py:20
  698.1 23.7 %collective-permute-start = (bf16[2,4,96,256]{2,1,0,3:T(4,128)(2,1)S(1)}, bf16[2,4,96,256]{2,1,0,3:T(4,128)(2,1)S(1)}, u32[]{:S(2)}, u32[]{:S(2)}) collective-permute-start(bf16[2,4,96,256]{2,1,0,3:T(4,128)(2,1)S(1)} %get-tuple-element.237), channel_id=1, source_target_pairs={{0,16},{16,32},{32,48},{48,64},{64,80},{80,96},{96,112},{112,128},... | collective-permute-start | bytes 1179656 | tf_op jit(solution)/shard_map/while/body/eval_jaxpr/ppermute | solution.py:20
  727.5 24.9 %collective-permute-start = (bf16[2,4,96,256]{2,1,0,3:T(4,128)(2,1)S(1)}, bf16[2,4,96,256]{2,1,0,3:T(4,128)(2,1)S(1)}, u32[]{:S(2)}, u32[]{:S(2)}) collective-permute-start(bf16[2,4,96,256]{2,1,0,3:T(4,128)(2,1)S(1)} %get-tuple-element.237), channel_id=1, source_target_pairs={{0,16},{16,32},{32,48},{48,64},{64,80},{80,96},{96,112},{112,128},... | collective-permute-start | bytes 1179656 | tf_op jit(solution)/shard_map/while/body/eval_jaxpr/ppermute | solution.py:20
  758.0 24.8 %collective-permute-start = (bf16[2,4,96,256]{2,1,0,3:T(4,128)(2,1)S(1)}, bf16[2,4,96,256]{2,1,0,3:T(4,128)(2,1)S(1)}, u32[]{:S(2)}, u32[]{:S(2)}) collective-permute-start(bf16[2,4,96,256]{2,1,0,3:T(4,128)(2,1)S(1)} %get-tuple-element.237), channel_id=1, source_target_pairs={{0,16},{16,32},{32,48},{48,64},{64,80},{80,96},{96,112},{112,128},... | collective-permute-start | bytes 1179656 | tf_op jit(solution)/shard_map/while/body/eval_jaxpr/ppermute | solution.py:20
  788.4 23.9 %collective-permute-start = (bf16[2,4,96,256]{2,1,0,3:T(4,128)(2,1)S(1)}, bf16[2,4,96,256]{2,1,0,3:T(4,128)(2,1)S(1)}, u32[]{:S(2)}, u32[]{:S(2)}) collective-permute-start(bf16[2,4,96,256]{2,1,0,3:T(4,128)(2,1)S(1)} %get-tuple-element.237), channel_id=1, source_target_pairs={{0,16},{16,32},{32,48},{48,64},{64,80},{80,96},{96,112},{112,128},... | collective-permute-start | bytes 1179656 | tf_op jit(solution)/shard_map/while/body/eval_jaxpr/ppermute | solution.py:20
  818.0 23.0 %collective-permute-start = (bf16[2,4,96,256]{2,1,0,3:T(4,128)(2,1)S(1)}, bf16[2,4,96,256]{2,1,0,3:T(4,128)(2,1)S(1)}, u32[]{:S(2)}, u32[]{:S(2)}) collective-permute-start(bf16[2,4,96,256]{2,1,0,3:T(4,128)(2,1)S(1)} %get-tuple-element.237), channel_id=1, source_target_pairs={{0,16},{16,32},{32,48},{48,64},{64,80},{80,96},{96,112},{112,128},... | collective-permute-start | bytes 1179656 | tf_op jit(solution)/shard_map/while/body/eval_jaxpr/ppermute | solution.py:20
  846.7 22.1 %collective-permute-start = (bf16[2,4,96,256]{2,1,0,3:T(4,128)(2,1)S(1)}, bf16[2,4,96,256]{2,1,0,3:T(4,128)(2,1)S(1)}, u32[]{:S(2)}, u32[]{:S(2)}) collective-permute-start(bf16[2,4,96,256]{2,1,0,3:T(4,128)(2,1)S(1)} %get-tuple-element.237), channel_id=1, source_target_pairs={{0,16},{16,32},{32,48},{48,64},{64,80},{80,96},{96,112},{112,128},... | collective-permute-start | bytes 1179656 | tf_op jit(solution)/shard_map/while/body/eval_jaxpr/ppermute | solution.py:20
  874.5 21.2 %collective-permute-start = (bf16[2,4,96,256]{2,1,0,3:T(4,128)(2,1)S(1)}, bf16[2,4,96,256]{2,1,0,3:T(4,128)(2,1)S(1)}, u32[]{:S(2)}, u32[]{:S(2)}) collective-permute-start(bf16[2,4,96,256]{2,1,0,3:T(4,128)(2,1)S(1)} %get-tuple-element.237), channel_id=1, source_target_pairs={{0,16},{16,32},{32,48},{48,64},{64,80},{80,96},{96,112},{112,128},... | collective-permute-start | bytes 1179656 | tf_op jit(solution)/shard_map/while/body/eval_jaxpr/ppermute | solution.py:20
  901.3 20.3 %collective-permute-start = (bf16[2,4,96,256]{2,1,0,3:T(4,128)(2,1)S(1)}, bf16[2,4,96,256]{2,1,0,3:T(4,128)(2,1)S(1)}, u32[]{:S(2)}, u32[]{:S(2)}) collective-permute-start(bf16[2,4,96,256]{2,1,0,3:T(4,128)(2,1)S(1)} %get-tuple-element.237), channel_id=1, source_target_pairs={{0,16},{16,32},{32,48},{48,64},{64,80},{80,96},{96,112},{112,128},... | collective-permute-start | bytes 1179656 | tf_op jit(solution)/shard_map/while/body/eval_jaxpr/ppermute | solution.py:20
  927.2 19.8 %collective-permute-start = (bf16[2,4,96,256]{2,1,0,3:T(4,128)(2,1)S(1)}, bf16[2,4,96,256]{2,1,0,3:T(4,128)(2,1)S(1)}, u32[]{:S(2)}, u32[]{:S(2)}) collective-permute-start(bf16[2,4,96,256]{2,1,0,3:T(4,128)(2,1)S(1)} %get-tuple-element.237), channel_id=1, source_target_pairs={{0,16},{16,32},{32,48},{48,64},{64,80},{80,96},{96,112},{112,128},... | collective-permute-start | bytes 1179656 | tf_op jit(solution)/shard_map/while/body/eval_jaxpr/ppermute | solution.py:20
  952.7 19.8 %collective-permute-start = (bf16[2,4,96,256]{2,1,0,3:T(4,128)(2,1)S(1)}, bf16[2,4,96,256]{2,1,0,3:T(4,128)(2,1)S(1)}, u32[]{:S(2)}, u32[]{:S(2)}) collective-permute-start(bf16[2,4,96,256]{2,1,0,3:T(4,128)(2,1)S(1)} %get-tuple-element.237), channel_id=1, source_target_pairs={{0,16},{16,32},{32,48},{48,64},{64,80},{80,96},{96,112},{112,128},... | collective-permute-start | bytes 1179656 | tf_op jit(solution)/shard_map/while/body/eval_jaxpr/ppermute | solution.py:20
  978.1 1.0 copy-start
